TPU v7x, 768 devices: a whole 4x8x12 slice. The times are simulated.
768 devices in a mesh: blk: 192 (over x_lo, y, z), group: 4 (over x_hi, core).
Axes of the slice: x: 4 (x_hi: 2, x_lo: 2; x = x_hi * 2 + x_lo), y: 8, z: 12, core: 2. Of those that a mesh axis runs over, the one named last changes fastest.
Arguments:
- photo_features: float32 [122880, 1152], P(('blk', 'group')), may hold values from -0.1875 to 0.1875
- text_emb: float32 [122880, 1152], P(('blk', 'group')), may hold values from -0.1875 to 0.1875
- sharpness_factor: float32 [1], replicated, may hold values from 30 to 100
- logit_bias: float32 [1], replicated, may hold values from -6 to -2
Outputs:
- photo_feature_derivative: float32 [122880, 1152], P(('blk', 'group'))
- sentence_feature_derivative: float32 [122880, 1152], P(('blk', 'group'))
All inputs are finite; a program needn't handle non-finite values.
Results may differ from a plain program's by a relative error of at most 0.0003.
Values sent between devices are 32-bit elements; how exact they have to be, the bound alone decides.
No kernel may reach another device: no remote copies, remote signals or barrier semaphores. Data moves between devices by JAX's collectives and lax.ppermute only.
A program may use at most 64 MiB of HBM per device.

v0:
```python
import jax
import jax.numpy as jnp
from jax import lax
from jax.sharding import PartitionSpec as P

AXES = ("blk", "group")


def routes(mesh):
    positions, members = mesh.shape["blk"], mesh.shape["group"]
    forward, across, sibling = [], [], []
    for b in range(positions):
        for g in range(members):
            half, core = divmod(g, 2)
            turn = (b + 1) % (positions // 2) == 0
            landing = (1 - half if turn and core == 1 else half) * 2 + core
            here = b * members + g
            forward.append((here, (b + 1) % positions * members + landing))
            across.append((here, b * members + (1 - half) * 2 + core))
            sibling.append((here, b * members + half * 2 + 1 - core))
    backward = [(target, source) for source, target in forward]
    return forward, backward, across, sibling


def dot(a, b, dims):
    return lax.dot_general(a, b, (dims, ((), ())), precision=lax.Precision.HIGH, preferred_element_type=jnp.float32)


def after(value, *earlier):
    return lax.optimization_barrier((value, *earlier))[0]


def solution(mesh):
    forward, backward, across, sibling = routes(mesh)

    def move(x, pairs):
        return lax.ppermute(x, AXES, pairs)

    def shards(photo, text, sharpness, bias):
        rows = photo.shape[0]
        scale, offset = sharpness[0], bias[0]
        text_f = move(text, forward)
        text_b = move(text, backward)
        far = move(photo, across)
        near = move(photo, sibling)
        far_near = move(far, sibling)
        texts = jnp.concatenate([text, text_f, text_b], axis=0)
        p = jnp.concatenate([photo, far, far_near, near], axis=0)
        r = jnp.arange(4 * rows, dtype=jnp.int32)[:, None]
        c = jnp.arange(3 * rows, dtype=jnp.int32)[None, :]
        label = jnp.where((r == c) & (r < rows), jnp.float32(1), jnp.float32(-1))
        logit = scale * dot(p, texts, ((1,), (1,))) + offset
        g = -label * jax.nn.sigmoid(-label * logit) * scale
        p_far = dot(g[rows : 3 * rows], texts, ((1,), (0,)))
        far_near_back = move(p_far[rows:], sibling)
        t_fb = dot(after(g, p_far)[:, rows:], p, ((0,), (0,)))
        b_back = move(t_fb[rows:], forward)
        p_across = p_far[:rows] + after(far_near_back, t_fb)
        far_back = move(p_across, across)
        f_back = move(after(t_fb[:rows], p_across), backward)
        g = after(g, p_across)
        p_near = dot(g[3 * rows :], texts, ((1,), (0,)))
        near_back = move(p_near, sibling)
        g = after(g, p_near)
        p_own = dot(g[:rows], texts, ((1,), (0,)))
        t_own = dot(after(g, p_own)[:, :rows], p, ((0,), (0,)))
        t_own, b_back, far_back, f_back = lax.optimization_barrier((t_own, b_back, far_back, f_back))
        return p_own + near_back + far_back, t_own + b_back + f_back

    spec = P(AXES, None)
    return jax.shard_map(shards, mesh=mesh, in_specs=(spec, spec, P(), P()), out_specs=(spec, spec), check_vma=False)
```

profile of v0, /device:TPU:1, one launch (start us, length us, event | category | flops | bytes accessed | tf_op | source)
XLA Modules:
  0.0 88.4 jit_solution(14022106636507868213)
XLA Ops:
  0.6 5.5 %collective-permute-start = (f32[160,1152]{1,0:T(8,128)}, f32[160,1152]{1,0:T(8,128)S(1)}, u32[]{:S(2)}, u32[]{:S(2)}) collective-permute-start(f32[160,1152]{1,0:T(8,128)} %param.4), channel_id=1, source_target_pairs={{0,2},{1,3},{2,0},{3,1},{4,6},{5,7},{6,4},{7,5},{8,10},{9,11},{10,... | collective-permute-start | bytes 2211848 | tf_op jit(solution)/shard_map/ppermute | solution.py:37
  6.1 8.9 %collective-permute-start.2 = (f32[160,1152]{1,0:T(8,128)}, f32[160,1152]{1,0:T(8,128)S(1)}, u32[]{:S(2)}, u32[]{:S(2)}) collective-permute-start(f32[160,1152]{1,0:T(8,128)} %param.4), channel_id=1, source_target_pairs={{0,1},{1,0},{2,3},{3,2},{4,5},{5,4},{6,7},{7,6},{8,9},{9,8},{10,11... | collective-permute-start | bytes 2211848 | tf_op jit(solution)/shard_map/ppermute | solution.py:37
  15.0 1.9 %collective-permute-start.3 = (f32[160,1152]{1,0:T(8,128)}, f32[160,1152]{1,0:T(8,128)S(1)}, u32[]{:S(2)}, u32[]{:S(2)}) collective-permute-start(f32[160,1152]{1,0:T(8,128)} %param.5), channel_id=1, source_target_pairs={{0,4},{1,5},{2,6},{3,7},{4,8},{5,9},{6,10},{7,11},{8,12},{9,13},{1... | collective-permute-start | bytes 2211848 | tf_op jit(solution)/shard_map/ppermute | solution.py:37
  16.9 11.8 %collective-permute-start.4 = (f32[160,1152]{1,0:T(8,128)}, f32[160,1152]{1,0:T(8,128)S(1)}, u32[]{:S(2)}, u32[]{:S(2)}) collective-permute-start(f32[160,1152]{1,0:T(8,128)} %param.5), channel_id=1, source_target_pairs={{4,0},{5,1},{6,2},{7,3},{8,4},{9,5},{10,6},{11,7},{12,8},{13,9},{1... | collective-permute-start | bytes 2211848 | tf_op jit(solution)/shard_map/ppermute | solution.py:37
  30.0 1.2 %constant_dynamic-update-slice_fusion.6 = f32[480,1152]{1,0:T(8,128)S(1)} fusion(f32[160,1152]{1,0:T(8,128)} %param.5), kind=kLoop, calls=%fused_computation.30 | loop fusion | bytes 1474560
  31.2 1.2 %constant_dynamic-update-slice_fusion.3 = f32[640,1152]{1,0:T(8,128)S(1)} fusion(f32[160,1152]{1,0:T(8,128)} %param.4), kind=kLoop, calls=%fused_computation.27 | loop fusion | bytes 1474560
  32.4 0.0 collective-permute-done
  32.4 1.9 %collective-permute-start.1 = (f32[160,1152]{1,0:T(8,128)S(1)}, f32[160,1152]{1,0:T(8,128)S(1)}, u32[]{:S(2)}, u32[]{:S(2)}) collective-permute-start(f32[160,1152]{1,0:T(8,128)S(1)} %collective-permute-done), channel_id=1, source_target_pairs={{0,1},{1,0},{2,3},{3,2},{4,5},{5,4},{6,7},{7,6},{8,9},{9,8},{10,11... | collective-permute-start | bytes 2211848 | tf_op jit(solution)/shard_map/ppermute | solution.py:37
  34.3 0.1 constant_dynamic-update-slice_fusion.2
  34.4 9.2 %collective-permute-done.3 = f32[160,1152]{1,0:T(8,128)S(1)} collective-permute-done((f32[160,1152]{1,0:T(8,128)}, f32[160,1152]{1,0:T(8,128)S(1)}, u32[]{:S(2)}, u32[]{:S(2)}) %collective-permute-start.3) | collective-permute-done | bytes 737312 | tf_op jit(solution)/shard_map/ppermute | solution.py:37
  43.6 1.7 %collective-permute-done.4 = f32[160,1152]{1,0:T(8,128)S(1)} collective-permute-done((f32[160,1152]{1,0:T(8,128)}, f32[160,1152]{1,0:T(8,128)S(1)}, u32[]{:S(2)}, u32[]{:S(2)}) %collective-permute-start.4) | collective-permute-done | bytes 737312 | tf_op jit(solution)/shard_map/ppermute | solution.py:37
  45.3 0.0 collective-permute-done.1
  45.3 0.1 constant_dynamic-update-slice_fusion.1
  45.4 0.0 collective-permute-done.2
  45.4 0.1 constant_dynamic-update-slice_fusion
  45.5 3.2 %fusion.7 = f32[640,480]{0,1:T(8,128)S(1)} fusion(f32[640,1152]{1,0:T(8,128)S(1)} %constant_dynamic-update-slice_fusion, f32[480,1152]{1,0:T(8,128)S(1)} %constant_dynamic-update-slice_fusion.4, f32[]{:T(128)} %bitcast.10, f32[]{:T(128)} %bitcast.9, pred[640]{0:T(1024)(128)(4,1)S(1)} %iota_compare_fusion.1), kind=kOutput, calls=%fused_computation.8 | convolution fusion | flops 2127052800 | bytes 6390408 | tf_op jit(solution)/shard_map/dot_general | solution.py:26
  48.6 1.9 %fusion.11 = f32[320,1152]{1,0:T(8,128)S(1)} fusion(f32[480,1152]{1,0:T(8,128)S(1)} %constant_dynamic-update-slice_fusion.4, f32[640,480]{0,1:T(8,128)S(1)} %fusion.7), kind=kOutput, calls=%fused_computation.14 | convolution fusion | flops 1061683200 | bytes 4423680 | tf_op jit(solution)/shard_map/dot_general | solution.py:26
  50.6 2.2 %collective-permute-start.5 = (f32[160,1152]{1,0:T(8,128)S(1)}, f32[160,1152]{1,0:T(8,128)S(1)}, u32[]{:S(2)}, u32[]{:S(2)}) collective-permute-start(f32[160,1152]{1,0:T(8,128)S(1)} %slice.38), channel_id=1, source_target_pairs={{0,1},{1,0},{2,3},{3,2},{4,5},{5,4},{6,7},{7,6},{8,9},{9,8},{10,11... | collective-permute-start | bytes 2211848 | tf_op jit(solution)/shard_map/ppermute | solution.py:37
  52.9 2.3 %fusion.9 = f32[320,1152]{1,0:T(8,128)S(1)} fusion(f32[640,1152]{1,0:T(8,128)S(1)} %constant_dynamic-update-slice_fusion, f32[640,480]{0,1:T(8,128)S(1)} %fusion.7), kind=kOutput, calls=%fused_computation.11 | convolution fusion | flops 1415577600 | bytes 5242880 | tf_op jit(solution)/shard_map/dot_general | solution.py:26
  55.2 0.1 fusion.19
  55.3 1.9 %collective-permute-start.7 = (f32[160,1152]{1,0:T(8,128)S(1)}, f32[160,1152]{1,0:T(8,128)S(1)}, u32[]{:S(2)}, u32[]{:S(2)}) collective-permute-start(f32[160,1152]{1,0:T(8,128)S(1)} %get-tuple-element.23), channel_id=1, source_target_pairs={{0,4},{1,5},{2,6},{3,7},{4,8},{5,9},{6,10},{7,11},{8,12},{9,13},{1... | collective-permute-start | bytes 2211848 | tf_op jit(solution)/shard_map/ppermute | solution.py:37
  57.2 0.0 collective-permute-done.5
  57.2 0.1 slice_add_fusion
  57.3 3.3 %collective-permute-start.8 = (f32[160,1152]{1,0:T(8,128)S(1)}, f32[160,1152]{1,0:T(8,128)S(1)}, u32[]{:S(2)}, u32[]{:S(2)}) collective-permute-start(f32[160,1152]{1,0:T(8,128)S(1)} %slice_add_fusion), channel_id=1, source_target_pairs={{0,2},{1,3},{2,0},{3,1},{4,6},{5,7},{6,4},{7,5},{8,10},{9,11},{10,... | collective-permute-start | bytes 2211848 | tf_op jit(solution)/shard_map/ppermute | solution.py:37
  60.6 9.2 %collective-permute-start.9 = (f32[160,1152]{1,0:T(8,128)S(1)}, f32[160,1152]{1,0:T(8,128)S(1)}, u32[]{:S(2)}, u32[]{:S(2)}) collective-permute-start(f32[160,1152]{1,0:T(8,128)S(1)} %get-tuple-element.17), channel_id=1, source_target_pairs={{4,0},{5,1},{6,2},{7,3},{8,4},{9,5},{10,6},{11,7},{12,8},{13,9},{1... | collective-permute-start | bytes 2211848 | tf_op jit(solution)/shard_map/ppermute | solution.py:37
  69.8 1.2 %fusion.15 = f32[160,1152]{1,0:T(8,128)S(1)} fusion(f32[480,1152]{1,0:T(8,128)S(1)} %constant_dynamic-update-slice_fusion.4, f32[640,480]{0,1:T(8,128)S(1)} %fusion.7), kind=kOutput, calls=%fused_computation.20 | convolution fusion | flops 530841600 | bytes 3440640 | tf_op jit(solution)/shard_map/dot_general | solution.py:26
  71.0 2.1 %collective-permute-start.6 = (f32[160,1152]{1,0:T(8,128)S(1)}, f32[160,1152]{1,0:T(8,128)S(1)}, u32[]{:S(2)}, u32[]{:S(2)}) collective-permute-start(f32[160,1152]{1,0:T(8,128)S(1)} %fusion.15), channel_id=1, source_target_pairs={{0,1},{1,0},{2,3},{3,2},{4,5},{5,4},{6,7},{7,6},{8,9},{9,8},{10,11... | collective-permute-start | bytes 2211848 | tf_op jit(solution)/shard_map/ppermute | solution.py:37
  73.2 1.0 %fusion.13 = f32[160,1152]{1,0:T(8,128)S(1)} fusion(f32[480,1152]{1,0:T(8,128)S(1)} %constant_dynamic-update-slice_fusion.4, f32[640,480]{0,1:T(8,128)S(1)} %fusion.7), kind=kOutput, calls=%fused_computation.18 | convolution fusion | flops 530841600 | bytes 3440640 | tf_op jit(solution)/shard_map/dot_general | solution.py:26
  74.2 1.4 %fusion.17 = f32[160,1152]{1,0:T(8,128)S(1)} fusion(f32[640,1152]{1,0:T(8,128)S(1)} %constant_dynamic-update-slice_fusion, f32[640,480]{0,1:T(8,128)S(1)} %fusion.7), kind=kOutput, calls=%fused_computation.22 | convolution fusion | flops 707788800 | bytes 4096000 | tf_op jit(solution)/shard_map/dot_general | solution.py:26
  75.6 5.3 %collective-permute-done.7 = f32[160,1152]{1,0:T(8,128)S(1)} collective-permute-done((f32[160,1152]{1,0:T(8,128)S(1)}, f32[160,1152]{1,0:T(8,128)S(1)}, u32[]{:S(2)}, u32[]{:S(2)}) %collective-permute-start.7) | collective-permute-done | bytes 737312 | tf_op jit(solution)/shard_map/ppermute | solution.py:37
  80.9 5.6 %collective-permute-done.8 = f32[160,1152]{1,0:T(8,128)S(1)} collective-permute-done((f32[160,1152]{1,0:T(8,128)S(1)}, f32[160,1152]{1,0:T(8,128)S(1)}, u32[]{:S(2)}, u32[]{:S(2)}) %collective-permute-start.8) | collective-permute-done | bytes 737312 | tf_op jit(solution)/shard_map/ppermute | solution.py:37
  86.5 0.0 collective-permute-done.9
  86.5 1.0 %add_add_fusion = f32[160,1152]{1,0:T(8,128)} fusion(f32[160,1152]{1,0:T(8,128)S(1)} %collective-permute-done.9, f32[160,1152]{1,0:T(8,128)S(1)} %fusion.17, f32[160,1152]{1,0:T(8,128)S(1)} %collective-permute-done.7), kind=kLoop, calls=%fused_computation.16 | loop fusion | flops 368640 | bytes 2949120 | tf_op jit(solution)/shard_map/add | solution.py:68
  87.5 0.0 collective-permute-done.6
  87.5 1.0 %add_add_fusion.1 = f32[160,1152]{1,0:T(8,128)} fusion(f32[160,1152]{1,0:T(8,128)S(1)} %collective-permute-done.8, f32[160,1152]{1,0:T(8,128)S(1)} %fusion.13, f32[160,1152]{1,0:T(8,128)S(1)} %collective-permute-done.6), kind=kLoop, calls=%fused_computation.17 | loop fusion | flops 368640 | bytes 2949120 | tf_op jit(solution)/shard_map/add | solution.py:68
  (4 shorter events, 0.2 us)
Async XLA Ops:
  0.6 31.7 %collective-permute-start = (f32[160,1152]{1,0:T(8,128)}, f32[160,1152]{1,0:T(8,128)S(1)}, u32[]{:S(2)}, u32[]{:S(2)}) collective-permute-start(f32[160,1152]{1,0:T(8,128)} %param.4), channel_id=1, source_target_pairs={{0,2},{1,3},{2,0},{3,1},{4,6},{5,7},{6,4},{7,5},{8,10},{9,11},{10,... | collective-permute-start | bytes 2211848 | tf_op jit(solution)/shard_map/ppermute | solution.py:37
  6.1 39.3 %collective-permute-start.2 = (f32[160,1152]{1,0:T(8,128)}, f32[160,1152]{1,0:T(8,128)S(1)}, u32[]{:S(2)}, u32[]{:S(2)}) collective-permute-start(f32[160,1152]{1,0:T(8,128)} %param.4), channel_id=1, source_target_pairs={{0,1},{1,0},{2,3},{3,2},{4,5},{5,4},{6,7},{7,6},{8,9},{9,8},{10,11... | collective-permute-start | bytes 2211848 | tf_op jit(solution)/shard_map/ppermute | solution.py:37
  15.0 28.5 %collective-permute-start.3 = (f32[160,1152]{1,0:T(8,128)}, f32[160,1152]{1,0:T(8,128)S(1)}, u32[]{:S(2)}, u32[]{:S(2)}) collective-permute-start(f32[160,1152]{1,0:T(8,128)} %param.5), channel_id=1, source_target_pairs={{0,4},{1,5},{2,6},{3,7},{4,8},{5,9},{6,10},{7,11},{8,12},{9,13},{1... | collective-permute-start | bytes 2211848 | tf_op jit(solution)/shard_map/ppermute | solution.py:37
  16.9 28.3 %collective-permute-start.4 = (f32[160,1152]{1,0:T(8,128)}, f32[160,1152]{1,0:T(8,128)S(1)}, u32[]{:S(2)}, u32[]{:S(2)}) collective-permute-start(f32[160,1152]{1,0:T(8,128)} %param.5), channel_id=1, source_target_pairs={{4,0},{5,1},{6,2},{7,3},{8,4},{9,5},{10,6},{11,7},{12,8},{13,9},{1... | collective-permute-start | bytes 2211848 | tf_op jit(solution)/shard_map/ppermute | solution.py:37
  32.4 12.9 %collective-permute-start.1 = (f32[160,1152]{1,0:T(8,128)S(1)}, f32[160,1152]{1,0:T(8,128)S(1)}, u32[]{:S(2)}, u32[]{:S(2)}) collective-permute-start(f32[160,1152]{1,0:T(8,128)S(1)} %collective-permute-done), channel_id=1, source_target_pairs={{0,1},{1,0},{2,3},{3,2},{4,5},{5,4},{6,7},{7,6},{8,9},{9,8},{10,11... | collective-permute-start | bytes 2211848 | tf_op jit(solution)/shard_map/ppermute | solution.py:37
  50.6 6.6 %collective-permute-start.5 = (f32[160,1152]{1,0:T(8,128)S(1)}, f32[160,1152]{1,0:T(8,128)S(1)}, u32[]{:S(2)}, u32[]{:S(2)}) collective-permute-start(f32[160,1152]{1,0:T(8,128)S(1)} %slice.38), channel_id=1, source_target_pairs={{0,1},{1,0},{2,3},{3,2},{4,5},{5,4},{6,7},{7,6},{8,9},{9,8},{10,11... | collective-permute-start | bytes 2211848 | tf_op jit(solution)/shard_map/ppermute | solution.py:37
  55.3 25.7 %collective-permute-start.7 = (f32[160,1152]{1,0:T(8,128)S(1)}, f32[160,1152]{1,0:T(8,128)S(1)}, u32[]{:S(2)}, u32[]{:S(2)}) collective-permute-start(f32[160,1152]{1,0:T(8,128)S(1)} %get-tuple-element.23), channel_id=1, source_target_pairs={{0,4},{1,5},{2,6},{3,7},{4,8},{5,9},{6,10},{7,11},{8,12},{9,13},{1... | collective-permute-start | bytes 2211848 | tf_op jit(solution)/shard_map/ppermute | solution.py:37
  57.3 29.2 %collective-permute-start.8 = (f32[160,1152]{1,0:T(8,128)S(1)}, f32[160,1152]{1,0:T(8,128)S(1)}, u32[]{:S(2)}, u32[]{:S(2)}) collective-permute-start(f32[160,1152]{1,0:T(8,128)S(1)} %slice_add_fusion), channel_id=1, source_target_pairs={{0,2},{1,3},{2,0},{3,1},{4,6},{5,7},{6,4},{7,5},{8,10},{9,11},{10,... | collective-permute-start | bytes 2211848 | tf_op jit(solution)/shard_map/ppermute | solution.py:37
  60.6 25.9 %collective-permute-start.9 = (f32[160,1152]{1,0:T(8,128)S(1)}, f32[160,1152]{1,0:T(8,128)S(1)}, u32[]{:S(2)}, u32[]{:S(2)}) collective-permute-start(f32[160,1152]{1,0:T(8,128)S(1)} %get-tuple-element.17), channel_id=1, source_target_pairs={{4,0},{5,1},{6,2},{7,3},{8,4},{9,5},{10,6},{11,7},{12,8},{13,9},{1... | collective-permute-start | bytes 2211848 | tf_op jit(solution)/shard_map/ppermute | solution.py:37
  71.0 16.4 %collective-permute-start.6 = (f32[160,1152]{1,0:T(8,128)S(1)}, f32[160,1152]{1,0:T(8,128)S(1)}, u32[]{:S(2)}, u32[]{:S(2)}) collective-permute-start(f32[160,1152]{1,0:T(8,128)S(1)} %fusion.15), channel_id=1, source_target_pairs={{0,1},{1,0},{2,3},{3,2},{4,5},{5,4},{6,7},{7,6},{8,9},{9,8},{10,11... | collective-permute-start | bytes 2211848 | tf_op jit(solution)/shard_map/ppermute | solution.py:37
where the time goes:
time: 88.9 us; the launch traced here: 88.4 us
  starting transfers between devices  48.7 us (55%)
  waiting for transfers between devices  21.8 us (25%)
  matrix products  11 us (12%)
  local copies, waits for them, and re-layouts  2.73 us (3%)
  between operations  2.15 us (2%)
  other arithmetic  2.03 us (2%)
    ppermute x10, starting transfers between devices, move(): return lax.ppermute(x, AXES, pairs)  48.7 us
    ppermute x10, waiting for transfers between devices, move(): return lax.ppermute(x, AXES, pairs)  21.8 us
    dot_general x6, matrix products, dot(): lax.dot_general(a, b, (dims, ((), ())), precision=lax.Precision.HIGH, pre...  11 us
    unnamed x5, local copies, waits for them, and re-layouts  2.48 us
    add x2, other arithmetic, shards(): return (p_own + near_back + far_back, t_own + b_back + f_back)  1.94 us
  transfers between devices with their start and end apart: 10, of which 4 were waited for; matrix products, arithmetic and copies ran while one was open for 11% of the time, Pallas kernels for 0%

commit v1 on v0

--- a/solution.py
+++ b/solution.py
@@ -4,6 +4,7 @@
 from jax.sharding import PartitionSpec as P
 
 AXES = ("blk", "group")
+RING = 12
 
 
 def routes(mesh):
@@ -32,6 +33,17 @@
 
 def solution(mesh):
     forward, backward, across, sibling = routes(mesh)
+    members = mesh.shape["group"]
+
+    def parted(pairs, first):
+        return [pair for pair in pairs if first(*pair)], [pair for pair in pairs if not first(*pair)]
+
+    def wraps(source, target):
+        return {source // members % RING, target // members % RING} == {0, RING - 1}
+
+    forward_wrap, forward_in = parted(forward, wraps)
+    backward_wrap, backward_in = parted(backward, wraps)
+    across_first, across_rest = parted(across, lambda source, target: source // members % RING == 0)
 
     def move(x, pairs):
         return lax.ppermute(x, AXES, pairs)
@@ -54,18 +66,21 @@
         p_far = dot(g[rows : 3 * rows], texts, ((1,), (0,)))
         far_near_back = move(p_far[rows:], sibling)
         t_fb = dot(after(g, p_far)[:, rows:], p, ((0,), (0,)))
-        b_back = move(t_fb[rows:], forward)
         p_across = p_far[:rows] + after(far_near_back, t_fb)
-        far_back = move(p_across, across)
+        far_back = move(p_across, across_first)
+        b_back = move(after(t_fb[rows:], p_across), forward)
         f_back = move(after(t_fb[:rows], p_across), backward)
         g = after(g, p_across)
         p_near = dot(g[3 * rows :], texts, ((1,), (0,)))
+        far_back_rest = move(after(p_across, p_near), across_rest)
         near_back = move(p_near, sibling)
         g = after(g, p_near)
         p_own = dot(g[:rows], texts, ((1,), (0,)))
         t_own = dot(after(g, p_own)[:, :rows], p, ((0,), (0,)))
-        t_own, b_back, far_back, f_back = lax.optimization_barrier((t_own, b_back, far_back, f_back))
-        return p_own + near_back + far_back, t_own + b_back + f_back
+        t_sum = after(t_own, p_own) + after(b_back, far_back)
+        t_sum = t_sum + after(f_back, t_sum)
+        far_back_rest = after(far_back_rest, t_sum)
+        return p_own + near_back + far_back + far_back_rest, t_sum
 
     spec = P(AXES, None)
     return jax.shard_map(shards, mesh=mesh, in_specs=(spec, spec, P(), P()), out_specs=(spec, spec), check_vma=False)

time: 88.9 us -> 88 us (0.990)
  waiting for transfers between devices: 21.8 us -> 20.4 us
    ppermute x10 -> x11, waiting for transfers between devices: 21.8 us -> 20.4 us  [move(): return lax.ppermute(x, AXES, pairs)]
    ppermute x10 -> x11, starting transfers between devices: 48.7 us -> 49 us  [move(): return lax.ppermute(x, AXES, pairs)]
    add x2 -> x3, other arithmetic: 1.94 us -> 2.03 us  [the longest x1 0.99 us: shards(): return (p_own + near_back + far_back + far_back_rest, t_sum)]
  transfers between devices with their start and end apart: 10 -> 11, of which waited for: 4 -> 4; matrix products, arithmetic and copies ran while one was open for 11% -> 11% of each run, Pallas kernels for 0% -> 0%
where the time goes in v1:
time: 88 us; the launch traced here: 87.5 us
  starting transfers between devices  49 us (56%)
  waiting for transfers between devices  20.4 us (23%)
  matrix products  11 us (12%)
  local copies, waits for them, and re-layouts  2.73 us (3%)
  between operations  2.16 us (2%)
  other arithmetic  2.12 us (2%)
    ppermute x11, starting transfers between devices, move(): return lax.ppermute(x, AXES, pairs)  49 us
    ppermute x11, waiting for transfers between devices, move(): return lax.ppermute(x, AXES, pairs)  20.4 us
    dot_general x6, matrix products, dot(): lax.dot_general(a, b, (dims, ((), ())), precision=lax.Precision.HIGH, pre...  11 us
    unnamed x5, local copies, waits for them, and re-layouts  2.48 us
  transfers between devices with their start and end apart: 11, of which 4 were waited for; matrix products, arithmetic and copies ran while one was open for 11% of the time, Pallas kernels for 0%

profile of v1, /device:TPU:1, one launch (start us, length us, event | category | flops | bytes accessed | tf_op | source)
XLA Modules:
  0.0 87.5 jit_solution(4047294571478418010)
XLA Ops:
  0.6 5.5 %collective-permute-start = (f32[160,1152]{1,0:T(8,128)}, f32[160,1152]{1,0:T(8,128)S(1)}, u32[]{:S(2)}, u32[]{:S(2)}) collective-permute-start(f32[160,1152]{1,0:T(8,128)} %param.4), channel_id=1, source_target_pairs={{0,2},{1,3},{2,0},{3,1},{4,6},{5,7},{6,4},{7,5},{8,10},{9,11},{10,... | collective-permute-start | bytes 2211848 | tf_op jit(solution)/shard_map/ppermute | solution.py:49
  6.1 8.9 %collective-permute-start.2 = (f32[160,1152]{1,0:T(8,128)}, f32[160,1152]{1,0:T(8,128)S(1)}, u32[]{:S(2)}, u32[]{:S(2)}) collective-permute-start(f32[160,1152]{1,0:T(8,128)} %param.4), channel_id=1, source_target_pairs={{0,1},{1,0},{2,3},{3,2},{4,5},{5,4},{6,7},{7,6},{8,9},{9,8},{10,11... | collective-permute-start | bytes 2211848 | tf_op jit(solution)/shard_map/ppermute | solution.py:49
  15.0 1.9 %collective-permute-start.3 = (f32[160,1152]{1,0:T(8,128)}, f32[160,1152]{1,0:T(8,128)S(1)}, u32[]{:S(2)}, u32[]{:S(2)}) collective-permute-start(f32[160,1152]{1,0:T(8,128)} %param.5), channel_id=1, source_target_pairs={{0,4},{1,5},{2,6},{3,7},{4,8},{5,9},{6,10},{7,11},{8,12},{9,13},{1... | collective-permute-start | bytes 2211848 | tf_op jit(solution)/shard_map/ppermute | solution.py:49
  16.9 11.8 %collective-permute-start.4 = (f32[160,1152]{1,0:T(8,128)}, f32[160,1152]{1,0:T(8,128)S(1)}, u32[]{:S(2)}, u32[]{:S(2)}) collective-permute-start(f32[160,1152]{1,0:T(8,128)} %param.5), channel_id=1, source_target_pairs={{4,0},{5,1},{6,2},{7,3},{8,4},{9,5},{10,6},{11,7},{12,8},{13,9},{1... | collective-permute-start | bytes 2211848 | tf_op jit(solution)/shard_map/ppermute | solution.py:49
  30.0 1.2 %constant_dynamic-update-slice_fusion.6 = f32[480,1152]{1,0:T(8,128)S(1)} fusion(f32[160,1152]{1,0:T(8,128)} %param.5), kind=kLoop, calls=%fused_computation.29 | loop fusion | bytes 1474560
  31.2 1.2 %constant_dynamic-update-slice_fusion.3 = f32[640,1152]{1,0:T(8,128)S(1)} fusion(f32[160,1152]{1,0:T(8,128)} %param.4), kind=kLoop, calls=%fused_computation.26 | loop fusion | bytes 1474560
  32.4 0.0 collective-permute-done
  32.4 1.9 %collective-permute-start.1 = (f32[160,1152]{1,0:T(8,128)S(1)}, f32[160,1152]{1,0:T(8,128)S(1)}, u32[]{:S(2)}, u32[]{:S(2)}) collective-permute-start(f32[160,1152]{1,0:T(8,128)S(1)} %collective-permute-done), channel_id=1, source_target_pairs={{0,1},{1,0},{2,3},{3,2},{4,5},{5,4},{6,7},{7,6},{8,9},{9,8},{10,11... | collective-permute-start | bytes 2211848 | tf_op jit(solution)/shard_map/ppermute | solution.py:49
  34.3 0.1 constant_dynamic-update-slice_fusion.2
  34.4 9.2 %collective-permute-done.3 = f32[160,1152]{1,0:T(8,128)S(1)} collective-permute-done((f32[160,1152]{1,0:T(8,128)}, f32[160,1152]{1,0:T(8,128)S(1)}, u32[]{:S(2)}, u32[]{:S(2)}) %collective-permute-start.3) | collective-permute-done | bytes 737312 | tf_op jit(solution)/shard_map/ppermute | solution.py:49
  43.6 1.7 %collective-permute-done.4 = f32[160,1152]{1,0:T(8,128)S(1)} collective-permute-done((f32[160,1152]{1,0:T(8,128)}, f32[160,1152]{1,0:T(8,128)S(1)}, u32[]{:S(2)}, u32[]{:S(2)}) %collective-permute-start.4) | collective-permute-done | bytes 737312 | tf_op jit(solution)/shard_map/ppermute | solution.py:49
  45.3 0.0 collective-permute-done.1
  45.3 0.1 constant_dynamic-update-slice_fusion.1
  45.4 0.0 collective-permute-done.2
  45.4 0.1 constant_dynamic-update-slice_fusion
  45.5 3.2 %fusion.7 = f32[640,480]{0,1:T(8,128)S(1)} fusion(f32[640,1152]{1,0:T(8,128)S(1)} %constant_dynamic-update-slice_fusion, f32[480,1152]{1,0:T(8,128)S(1)} %constant_dynamic-update-slice_fusion.4, f32[]{:T(128)} %bitcast.10, f32[]{:T(128)} %bitcast.9, pred[640]{0:T(1024)(128)(4,1)S(1)} %iota_compare_fusion.1), kind=kOutput, calls=%fused_computation.8 | convolution fusion | flops 2127052800 | bytes 6390408 | tf_op jit(solution)/shard_map/dot_general | solution.py:27
  48.6 1.9 %fusion.11 = f32[320,1152]{1,0:T(8,128)S(1)} fusion(f32[480,1152]{1,0:T(8,128)S(1)} %constant_dynamic-update-slice_fusion.4, f32[640,480]{0,1:T(8,128)S(1)} %fusion.7), kind=kOutput, calls=%fused_computation.14 | convolution fusion | flops 1061683200 | bytes 4423680 | tf_op jit(solution)/shard_map/dot_general | solution.py:27
  50.6 2.2 %collective-permute-start.5 = (f32[160,1152]{1,0:T(8,128)S(1)}, f32[160,1152]{1,0:T(8,128)S(1)}, u32[]{:S(2)}, u32[]{:S(2)}) collective-permute-start(f32[160,1152]{1,0:T(8,128)S(1)} %slice.38), channel_id=1, source_target_pairs={{0,1},{1,0},{2,3},{3,2},{4,5},{5,4},{6,7},{7,6},{8,9},{9,8},{10,11... | collective-permute-start | bytes 2211848 | tf_op jit(solution)/shard_map/ppermute | solution.py:49
  52.9 2.3 %fusion.9 = f32[320,1152]{1,0:T(8,128)S(1)} fusion(f32[640,1152]{1,0:T(8,128)S(1)} %constant_dynamic-update-slice_fusion, f32[640,480]{0,1:T(8,128)S(1)} %fusion.7), kind=kOutput, calls=%fused_computation.11 | convolution fusion | flops 1415577600 | bytes 5242880 | tf_op jit(solution)/shard_map/dot_general | solution.py:27
  55.2 0.1 fusion.19
  55.3 0.0 collective-permute-done.5
  55.3 0.1 slice_add_fusion
  55.4 3.3 %collective-permute-start.7 = (f32[160,1152]{1,0:T(8,128)S(1)}, f32[160,1152]{1,0:T(8,128)S(1)}, u32[]{:S(2)}, u32[]{:S(2)}) collective-permute-start(f32[160,1152]{1,0:T(8,128)S(1)} %slice_add_fusion), channel_id=1, source_target_pairs={{0,2},{1,3},{2,0},{3,1},{48,50},{49,51},{50,48},{51,49},{96,98},{9... | collective-permute-start | bytes 2211848 | tf_op jit(solution)/shard_map/ppermute | solution.py:49
  58.7 1.9 %collective-permute-start.9 = (f32[160,1152]{1,0:T(8,128)S(1)}, f32[160,1152]{1,0:T(8,128)S(1)}, u32[]{:S(2)}, u32[]{:S(2)}) collective-permute-start(f32[160,1152]{1,0:T(8,128)S(1)} %get-tuple-element.21), channel_id=1, source_target_pairs={{0,4},{1,5},{2,6},{3,7},{4,8},{5,9},{6,10},{7,11},{8,12},{9,13},{1... | collective-permute-start | bytes 2211848 | tf_op jit(solution)/shard_map/ppermute | solution.py:49
  60.6 8.8 %collective-permute-start.10 = (f32[160,1152]{1,0:T(8,128)S(1)}, f32[160,1152]{1,0:T(8,128)S(1)}, u32[]{:S(2)}, u32[]{:S(2)}) collective-permute-start(f32[160,1152]{1,0:T(8,128)S(1)} %get-tuple-element.23), channel_id=1, source_target_pairs={{4,0},{5,1},{6,2},{7,3},{8,4},{9,5},{10,6},{11,7},{12,8},{13,9},{1... | collective-permute-start | bytes 2211848 | tf_op jit(solution)/shard_map/ppermute | solution.py:49
  69.4 1.2 %fusion.15 = f32[160,1152]{1,0:T(8,128)S(1)} fusion(f32[480,1152]{1,0:T(8,128)S(1)} %constant_dynamic-update-slice_fusion.4, f32[640,480]{0,1:T(8,128)S(1)} %fusion.7), kind=kOutput, calls=%fused_computation.19 | convolution fusion | flops 530841600 | bytes 3440640 | tf_op jit(solution)/shard_map/dot_general | solution.py:27
  70.6 0.7 collective-permute-start.8
  71.3 2.1 %collective-permute-start.6 = (f32[160,1152]{1,0:T(8,128)S(1)}, f32[160,1152]{1,0:T(8,128)S(1)}, u32[]{:S(2)}, u32[]{:S(2)}) collective-permute-start(f32[160,1152]{1,0:T(8,128)S(1)} %fusion.15), channel_id=1, source_target_pairs={{0,1},{1,0},{2,3},{3,2},{4,5},{5,4},{6,7},{7,6},{8,9},{9,8},{10,11... | collective-permute-start | bytes 2211848 | tf_op jit(solution)/shard_map/ppermute | solution.py:49
  73.4 1.0 %fusion.13 = f32[160,1152]{1,0:T(8,128)S(1)} fusion(f32[480,1152]{1,0:T(8,128)S(1)} %constant_dynamic-update-slice_fusion.4, f32[640,480]{0,1:T(8,128)S(1)} %fusion.7), kind=kOutput, calls=%fused_computation.17 | convolution fusion | flops 530841600 | bytes 3440640 | tf_op jit(solution)/shard_map/dot_general | solution.py:27
  74.5 1.4 %fusion.17 = f32[160,1152]{1,0:T(8,128)S(1)} fusion(f32[640,1152]{1,0:T(8,128)S(1)} %constant_dynamic-update-slice_fusion, f32[640,480]{0,1:T(8,128)S(1)} %fusion.7), kind=kOutput, calls=%fused_computation.21 | convolution fusion | flops 707788800 | bytes 4096000 | tf_op jit(solution)/shard_map/dot_general | solution.py:27
  75.9 9.2 %collective-permute-done.7 = f32[160,1152]{1,0:T(8,128)S(1)} collective-permute-done((f32[160,1152]{1,0:T(8,128)S(1)}, f32[160,1152]{1,0:T(8,128)S(1)}, u32[]{:S(2)}, u32[]{:S(2)}) %collective-permute-start.7) | collective-permute-done | bytes 737312 | tf_op jit(solution)/shard_map/ppermute | solution.py:49
  85.0 0.0 collective-permute-done.9
  85.0 0.1 add.33
  85.1 0.4 collective-permute-done.10
  85.5 1.0 %add.34 = f32[160,1152]{1,0:T(8,128)} add(f32[160,1152]{1,0:T(8,128)S(1)} %add.33, f32[160,1152]{1,0:T(8,128)S(1)} %collective-permute-done.10) | non-fusion elementwise | flops 184320 | bytes 2211840 | tf_op jit(solution)/shard_map/add | solution.py:81
  86.5 0.0 collective-permute-done.8
  86.5 0.0 collective-permute-done.6
  86.5 1.0 %add_add_fusion = f32[160,1152]{1,0:T(8,128)} fusion(f32[160,1152]{1,0:T(8,128)S(1)} %collective-permute-done.8, f32[160,1152]{1,0:T(8,128)S(1)} %collective-permute-done.7, f32[160,1152]{1,0:T(8,128)S(1)} %fusion.13, f32[160,1152]{1,0:T(8,128)S(1)} %collective-permute-done.6), kind=kLoop, calls=%fused_computation.16 | loop fusion | flops 552960 | bytes 3686400 | tf_op jit(solution)/shard_map/add | solution.py:83
  (4 shorter events, 0.2 us)
Async XLA Ops:
  0.6 31.7 %collective-permute-start = (f32[160,1152]{1,0:T(8,128)}, f32[160,1152]{1,0:T(8,128)S(1)}, u32[]{:S(2)}, u32[]{:S(2)}) collective-permute-start(f32[160,1152]{1,0:T(8,128)} %param.4), channel_id=1, source_target_pairs={{0,2},{1,3},{2,0},{3,1},{4,6},{5,7},{6,4},{7,5},{8,10},{9,11},{10,... | collective-permute-start | bytes 2211848 | tf_op jit(solution)/shard_map/ppermute | solution.py:49
  6.1 39.3 %collective-permute-start.2 = (f32[160,1152]{1,0:T(8,128)}, f32[160,1152]{1,0:T(8,128)S(1)}, u32[]{:S(2)}, u32[]{:S(2)}) collective-permute-start(f32[160,1152]{1,0:T(8,128)} %param.4), channel_id=1, source_target_pairs={{0,1},{1,0},{2,3},{3,2},{4,5},{5,4},{6,7},{7,6},{8,9},{9,8},{10,11... | collective-permute-start | bytes 2211848 | tf_op jit(solution)/shard_map/ppermute | solution.py:49
  15.0 28.5 %collective-permute-start.3 = (f32[160,1152]{1,0:T(8,128)}, f32[160,1152]{1,0:T(8,128)S(1)}, u32[]{:S(2)}, u32[]{:S(2)}) collective-permute-start(f32[160,1152]{1,0:T(8,128)} %param.5), channel_id=1, source_target_pairs={{0,4},{1,5},{2,6},{3,7},{4,8},{5,9},{6,10},{7,11},{8,12},{9,13},{1... | collective-permute-start | bytes 2211848 | tf_op jit(solution)/shard_map/ppermute | solution.py:49
  16.9 28.3 %collective-permute-start.4 = (f32[160,1152]{1,0:T(8,128)}, f32[160,1152]{1,0:T(8,128)S(1)}, u32[]{:S(2)}, u32[]{:S(2)}) collective-permute-start(f32[160,1152]{1,0:T(8,128)} %param.5), channel_id=1, source_target_pairs={{4,0},{5,1},{6,2},{7,3},{8,4},{9,5},{10,6},{11,7},{12,8},{13,9},{1... | collective-permute-start | bytes 2211848 | tf_op jit(solution)/shard_map/ppermute | solution.py:49
  32.4 12.9 %collective-permute-start.1 = (f32[160,1152]{1,0:T(8,128)S(1)}, f32[160,1152]{1,0:T(8,128)S(1)}, u32[]{:S(2)}, u32[]{:S(2)}) collective-permute-start(f32[160,1152]{1,0:T(8,128)S(1)} %collective-permute-done), channel_id=1, source_target_pairs={{0,1},{1,0},{2,3},{3,2},{4,5},{5,4},{6,7},{7,6},{8,9},{9,8},{10,11... | collective-permute-start | bytes 2211848 | tf_op jit(solution)/shard_map/ppermute | solution.py:49
  50.6 4.6 %collective-permute-start.5 = (f32[160,1152]{1,0:T(8,128)S(1)}, f32[160,1152]{1,0:T(8,128)S(1)}, u32[]{:S(2)}, u32[]{:S(2)}) collective-permute-start(f32[160,1152]{1,0:T(8,128)S(1)} %slice.38), channel_id=1, source_target_pairs={{0,1},{1,0},{2,3},{3,2},{4,5},{5,4},{6,7},{7,6},{8,9},{9,8},{10,11... | collective-permute-start | bytes 2211848 | tf_op jit(solution)/shard_map/ppermute | solution.py:49
  55.4 29.7 %collective-permute-start.7 = (f32[160,1152]{1,0:T(8,128)S(1)}, f32[160,1152]{1,0:T(8,128)S(1)}, u32[]{:S(2)}, u32[]{:S(2)}) collective-permute-start(f32[160,1152]{1,0:T(8,128)S(1)} %slice_add_fusion), channel_id=1, source_target_pairs={{0,2},{1,3},{2,0},{3,1},{48,50},{49,51},{50,48},{51,49},{96,98},{9... | collective-permute-start | bytes 2211848 | tf_op jit(solution)/shard_map/ppermute | solution.py:49
  58.7 26.4 %collective-permute-start.9 = (f32[160,1152]{1,0:T(8,128)S(1)}, f32[160,1152]{1,0:T(8,128)S(1)}, u32[]{:S(2)}, u32[]{:S(2)}) collective-permute-start(f32[160,1152]{1,0:T(8,128)S(1)} %get-tuple-element.21), channel_id=1, source_target_pairs={{0,4},{1,5},{2,6},{3,7},{4,8},{5,9},{6,10},{7,11},{8,12},{9,13},{1... | collective-permute-start | bytes 2211848 | tf_op jit(solution)/shard_map/ppermute | solution.py:49
  60.6 24.9 %collective-permute-start.10 = (f32[160,1152]{1,0:T(8,128)S(1)}, f32[160,1152]{1,0:T(8,128)S(1)}, u32[]{:S(2)}, u32[]{:S(2)}) collective-permute-start(f32[160,1152]{1,0:T(8,128)S(1)} %get-tuple-element.23), channel_id=1, source_target_pairs={{4,0},{5,1},{6,2},{7,3},{8,4},{9,5},{10,6},{11,7},{12,8},{13,9},{1... | collective-permute-start | bytes 2211848 | tf_op jit(solution)/shard_map/ppermute | solution.py:49
  70.6 15.9 %collective-permute-start.8 = (f32[160,1152]{1,0:T(8,128)S(1)}, f32[160,1152]{1,0:T(8,128)S(1)}, u32[]{:S(2)}, u32[]{:S(2)}) collective-permute-start(f32[160,1152]{1,0:T(8,128)S(1)} %slice_add_fusion), channel_id=1, source_target_pairs={{4,6},{5,7},{6,4},{7,5},{8,10},{9,11},{10,8},{11,9},{12,14},{13,15... | collective-permute-start | bytes 2211848 | tf_op jit(solution)/shard_map/ppermute | solution.py:49
  71.3 15.2 %collective-permute-start.6 = (f32[160,1152]{1,0:T(8,128)S(1)}, f32[160,1152]{1,0:T(8,128)S(1)}, u32[]{:S(2)}, u32[]{:S(2)}) collective-permute-start(f32[160,1152]{1,0:T(8,128)S(1)} %fusion.15), channel_id=1, source_target_pairs={{0,1},{1,0},{2,3},{3,2},{4,5},{5,4},{6,7},{7,6},{8,9},{9,8},{10,11... | collective-permute-start | bytes 2211848 | tf_op jit(solution)/shard_map/ppermute | solution.py:49

commit v2 on v1

--- a/solution.py
+++ b/solution.py
@@ -77,9 +77,11 @@
         g = after(g, p_near)
         p_own = dot(g[:rows], texts, ((1,), (0,)))
         t_own = dot(after(g, p_own)[:, :rows], p, ((0,), (0,)))
-        t_sum = after(t_own, p_own) + after(b_back, far_back)
+        t_own, p_own = lax.optimization_barrier((t_own, p_own))
+        t_sum = t_own + b_back
         t_sum = t_sum + after(f_back, t_sum)
-        far_back_rest = after(far_back_rest, t_sum)
+        far_back = after(far_back, t_sum)
+        far_back_rest = after(far_back_rest, far_back)
         return p_own + near_back + far_back + far_back_rest, t_sum
 
     spec = P(AXES, None)

time: 88 us -> 88 us (level)
  no operation moved by 1% of the time
where the time goes in v2:
time: 88 us; the launch traced here: 87.5 us
  starting transfers between devices  49 us (56%)
  waiting for transfers between devices  20.4 us (23%)
  matrix products  11 us (12%)
  local copies, waits for them, and re-layouts  2.73 us (3%)
  between operations  2.16 us (2%)
  other arithmetic  2.12 us (2%)
    ppermute x11, starting transfers between devices, move(): return lax.ppermute(x, AXES, pairs)  49 us
    ppermute x11, waiting for transfers between devices, move(): return lax.ppermute(x, AXES, pairs)  20.4 us
    dot_general x6, matrix products, dot(): lax.dot_general(a, b, (dims, ((), ())), precision=lax.Precision.HIGH, pre...  11 us
    unnamed x5, local copies, waits for them, and re-layouts  2.48 us
  transfers between devices with their start and end apart: 11, of which 4 were waited for; matrix products, arithmetic and copies ran while one was open for 11% of the time, Pallas kernels for 0%

profile of v2, /device:TPU:1, one launch (start us, length us, event | category | flops | bytes accessed | tf_op | source)
XLA Modules:
  0.0 87.5 jit_solution(9861971694620909356)
XLA Ops:
  0.6 5.5 %collective-permute-start = (f32[160,1152]{1,0:T(8,128)}, f32[160,1152]{1,0:T(8,128)S(1)}, u32[]{:S(2)}, u32[]{:S(2)}) collective-permute-start(f32[160,1152]{1,0:T(8,128)} %param.4), channel_id=1, source_target_pairs={{0,2},{1,3},{2,0},{3,1},{4,6},{5,7},{6,4},{7,5},{8,10},{9,11},{10,... | collective-permute-start | bytes 2211848 | tf_op jit(solution)/shard_map/ppermute | solution.py:49
  6.1 8.9 %collective-permute-start.2 = (f32[160,1152]{1,0:T(8,128)}, f32[160,1152]{1,0:T(8,128)S(1)}, u32[]{:S(2)}, u32[]{:S(2)}) collective-permute-start(f32[160,1152]{1,0:T(8,128)} %param.4), channel_id=1, source_target_pairs={{0,1},{1,0},{2,3},{3,2},{4,5},{5,4},{6,7},{7,6},{8,9},{9,8},{10,11... | collective-permute-start | bytes 2211848 | tf_op jit(solution)/shard_map/ppermute | solution.py:49
  15.0 1.9 %collective-permute-start.3 = (f32[160,1152]{1,0:T(8,128)}, f32[160,1152]{1,0:T(8,128)S(1)}, u32[]{:S(2)}, u32[]{:S(2)}) collective-permute-start(f32[160,1152]{1,0:T(8,128)} %param.5), channel_id=1, source_target_pairs={{0,4},{1,5},{2,6},{3,7},{4,8},{5,9},{6,10},{7,11},{8,12},{9,13},{1... | collective-permute-start | bytes 2211848 | tf_op jit(solution)/shard_map/ppermute | solution.py:49
  16.9 11.8 %collective-permute-start.4 = (f32[160,1152]{1,0:T(8,128)}, f32[160,1152]{1,0:T(8,128)S(1)}, u32[]{:S(2)}, u32[]{:S(2)}) collective-permute-start(f32[160,1152]{1,0:T(8,128)} %param.5), channel_id=1, source_target_pairs={{4,0},{5,1},{6,2},{7,3},{8,4},{9,5},{10,6},{11,7},{12,8},{13,9},{1... | collective-permute-start | bytes 2211848 | tf_op jit(solution)/shard_map/ppermute | solution.py:49
  30.0 1.2 %constant_dynamic-update-slice_fusion.6 = f32[480,1152]{1,0:T(8,128)S(1)} fusion(f32[160,1152]{1,0:T(8,128)} %param.5), kind=kLoop, calls=%fused_computation.29 | loop fusion | bytes 1474560
  31.2 1.2 %constant_dynamic-update-slice_fusion.3 = f32[640,1152]{1,0:T(8,128)S(1)} fusion(f32[160,1152]{1,0:T(8,128)} %param.4), kind=kLoop, calls=%fused_computation.26 | loop fusion | bytes 1474560
  32.4 0.0 collective-permute-done
  32.4 1.9 %collective-permute-start.1 = (f32[160,1152]{1,0:T(8,128)S(1)}, f32[160,1152]{1,0:T(8,128)S(1)}, u32[]{:S(2)}, u32[]{:S(2)}) collective-permute-start(f32[160,1152]{1,0:T(8,128)S(1)} %collective-permute-done), channel_id=1, source_target_pairs={{0,1},{1,0},{2,3},{3,2},{4,5},{5,4},{6,7},{7,6},{8,9},{9,8},{10,11... | collective-permute-start | bytes 2211848 | tf_op jit(solution)/shard_map/ppermute | solution.py:49
  34.3 0.1 constant_dynamic-update-slice_fusion.2
  34.4 9.2 %collective-permute-done.3 = f32[160,1152]{1,0:T(8,128)S(1)} collective-permute-done((f32[160,1152]{1,0:T(8,128)}, f32[160,1152]{1,0:T(8,128)S(1)}, u32[]{:S(2)}, u32[]{:S(2)}) %collective-permute-start.3) | collective-permute-done | bytes 737312 | tf_op jit(solution)/shard_map/ppermute | solution.py:49
  43.6 1.7 %collective-permute-done.4 = f32[160,1152]{1,0:T(8,128)S(1)} collective-permute-done((f32[160,1152]{1,0:T(8,128)}, f32[160,1152]{1,0:T(8,128)S(1)}, u32[]{:S(2)}, u32[]{:S(2)}) %collective-permute-start.4) | collective-permute-done | bytes 737312 | tf_op jit(solution)/shard_map/ppermute | solution.py:49
  45.3 0.0 collective-permute-done.1
  45.3 0.1 constant_dynamic-update-slice_fusion.1
  45.4 0.0 collective-permute-done.2
  45.4 0.1 constant_dynamic-update-slice_fusion
  45.5 3.2 %fusion.7 = f32[640,480]{0,1:T(8,128)S(1)} fusion(f32[640,1152]{1,0:T(8,128)S(1)} %constant_dynamic-update-slice_fusion, f32[480,1152]{1,0:T(8,128)S(1)} %constant_dynamic-update-slice_fusion.4, f32[]{:T(128)} %bitcast.10, f32[]{:T(128)} %bitcast.9, pred[640]{0:T(1024)(128)(4,1)S(1)} %iota_compare_fusion.1), kind=kOutput, calls=%fused_computation.8 | convolution fusion | flops 2127052800 | bytes 6390408 | tf_op jit(solution)/shard_map/dot_general | solution.py:27
  48.6 1.9 %fusion.11 = f32[320,1152]{1,0:T(8,128)S(1)} fusion(f32[480,1152]{1,0:T(8,128)S(1)} %constant_dynamic-update-slice_fusion.4, f32[640,480]{0,1:T(8,128)S(1)} %fusion.7), kind=kOutput, calls=%fused_computation.14 | convolution fusion | flops 1061683200 | bytes 4423680 | tf_op jit(solution)/shard_map/dot_general | solution.py:27
  50.6 2.2 %collective-permute-start.5 = (f32[160,1152]{1,0:T(8,128)S(1)}, f32[160,1152]{1,0:T(8,128)S(1)}, u32[]{:S(2)}, u32[]{:S(2)}) collective-permute-start(f32[160,1152]{1,0:T(8,128)S(1)} %slice.38), channel_id=1, source_target_pairs={{0,1},{1,0},{2,3},{3,2},{4,5},{5,4},{6,7},{7,6},{8,9},{9,8},{10,11... | collective-permute-start | bytes 2211848 | tf_op jit(solution)/shard_map/ppermute | solution.py:49
  52.9 2.3 %fusion.9 = f32[320,1152]{1,0:T(8,128)S(1)} fusion(f32[640,1152]{1,0:T(8,128)S(1)} %constant_dynamic-update-slice_fusion, f32[640,480]{0,1:T(8,128)S(1)} %fusion.7), kind=kOutput, calls=%fused_computation.11 | convolution fusion | flops 1415577600 | bytes 5242880 | tf_op jit(solution)/shard_map/dot_general | solution.py:27
  55.2 0.1 fusion.19
  55.3 0.0 collective-permute-done.5
  55.3 0.1 slice_add_fusion
  55.4 3.3 %collective-permute-start.7 = (f32[160,1152]{1,0:T(8,128)S(1)}, f32[160,1152]{1,0:T(8,128)S(1)}, u32[]{:S(2)}, u32[]{:S(2)}) collective-permute-start(f32[160,1152]{1,0:T(8,128)S(1)} %slice_add_fusion), channel_id=1, source_target_pairs={{0,2},{1,3},{2,0},{3,1},{48,50},{49,51},{50,48},{51,49},{96,98},{9... | collective-permute-start | bytes 2211848 | tf_op jit(solution)/shard_map/ppermute | solution.py:49
  58.7 1.9 %collective-permute-start.8 = (f32[160,1152]{1,0:T(8,128)S(1)}, f32[160,1152]{1,0:T(8,128)S(1)}, u32[]{:S(2)}, u32[]{:S(2)}) collective-permute-start(f32[160,1152]{1,0:T(8,128)S(1)} %get-tuple-element.22), channel_id=1, source_target_pairs={{0,4},{1,5},{2,6},{3,7},{4,8},{5,9},{6,10},{7,11},{8,12},{9,13},{1... | collective-permute-start | bytes 2211848 | tf_op jit(solution)/shard_map/ppermute | solution.py:49
  60.6 8.8 %collective-permute-start.9 = (f32[160,1152]{1,0:T(8,128)S(1)}, f32[160,1152]{1,0:T(8,128)S(1)}, u32[]{:S(2)}, u32[]{:S(2)}) collective-permute-start(f32[160,1152]{1,0:T(8,128)S(1)} %get-tuple-element.23), channel_id=1, source_target_pairs={{4,0},{5,1},{6,2},{7,3},{8,4},{9,5},{10,6},{11,7},{12,8},{13,9},{1... | collective-permute-start | bytes 2211848 | tf_op jit(solution)/shard_map/ppermute | solution.py:49
  69.4 1.2 %fusion.15 = f32[160,1152]{1,0:T(8,128)S(1)} fusion(f32[480,1152]{1,0:T(8,128)S(1)} %constant_dynamic-update-slice_fusion.4, f32[640,480]{0,1:T(8,128)S(1)} %fusion.7), kind=kOutput, calls=%fused_computation.19 | convolution fusion | flops 530841600 | bytes 3440640 | tf_op jit(solution)/shard_map/dot_general | solution.py:27
  70.6 0.7 collective-permute-start.10
  71.3 2.1 %collective-permute-start.6 = (f32[160,1152]{1,0:T(8,128)S(1)}, f32[160,1152]{1,0:T(8,128)S(1)}, u32[]{:S(2)}, u32[]{:S(2)}) collective-permute-start(f32[160,1152]{1,0:T(8,128)S(1)} %fusion.15), channel_id=1, source_target_pairs={{0,1},{1,0},{2,3},{3,2},{4,5},{5,4},{6,7},{7,6},{8,9},{9,8},{10,11... | collective-permute-start | bytes 2211848 | tf_op jit(solution)/shard_map/ppermute | solution.py:49
  73.4 1.0 %fusion.13 = f32[160,1152]{1,0:T(8,128)S(1)} fusion(f32[480,1152]{1,0:T(8,128)S(1)} %constant_dynamic-update-slice_fusion.4, f32[640,480]{0,1:T(8,128)S(1)} %fusion.7), kind=kOutput, calls=%fused_computation.17 | convolution fusion | flops 530841600 | bytes 3440640 | tf_op jit(solution)/shard_map/dot_general | solution.py:27
  74.5 1.4 %fusion.17 = f32[160,1152]{1,0:T(8,128)S(1)} fusion(f32[640,1152]{1,0:T(8,128)S(1)} %constant_dynamic-update-slice_fusion, f32[640,480]{0,1:T(8,128)S(1)} %fusion.7), kind=kOutput, calls=%fused_computation.21 | convolution fusion | flops 707788800 | bytes 4096000 | tf_op jit(solution)/shard_map/dot_general | solution.py:27
  75.9 8.8 %collective-permute-done.8 = f32[160,1152]{1,0:T(8,128)S(1)} collective-permute-done((f32[160,1152]{1,0:T(8,128)S(1)}, f32[160,1152]{1,0:T(8,128)S(1)}, u32[]{:S(2)}, u32[]{:S(2)}) %collective-permute-start.8) | collective-permute-done | bytes 737312 | tf_op jit(solution)/shard_map/ppermute | solution.py:49
  84.7 0.1 add.32
  84.8 0.7 collective-permute-done.9
  85.5 1.0 %add.33 = f32[160,1152]{1,0:T(8,128)} add(f32[160,1152]{1,0:T(8,128)S(1)} %add.32, f32[160,1152]{1,0:T(8,128)S(1)} %collective-permute-done.9) | non-fusion elementwise | flops 184320 | bytes 2211840 | tf_op jit(solution)/shard_map/add | solution.py:82
  86.5 0.0 collective-permute-done.7
  86.5 0.0 collective-permute-done.10
  86.5 0.0 collective-permute-done.6
  86.5 1.0 %add_add_fusion = f32[160,1152]{1,0:T(8,128)} fusion(f32[160,1152]{1,0:T(8,128)S(1)} %collective-permute-done.10, f32[160,1152]{1,0:T(8,128)S(1)} %collective-permute-done.7, f32[160,1152]{1,0:T(8,128)S(1)} %fusion.13, f32[160,1152]{1,0:T(8,128)S(1)} %collective-permute-done.6), kind=kLoop, calls=%fused_computation.16 | loop fusion | flops 552960 | bytes 3686400 | tf_op jit(solution)/shard_map/add | solution.py:85
  (4 shorter events, 0.2 us)
Async XLA Ops:
  0.6 31.7 %collective-permute-start = (f32[160,1152]{1,0:T(8,128)}, f32[160,1152]{1,0:T(8,128)S(1)}, u32[]{:S(2)}, u32[]{:S(2)}) collective-permute-start(f32[160,1152]{1,0:T(8,128)} %param.4), channel_id=1, source_target_pairs={{0,2},{1,3},{2,0},{3,1},{4,6},{5,7},{6,4},{7,5},{8,10},{9,11},{10,... | collective-permute-start | bytes 2211848 | tf_op jit(solution)/shard_map/ppermute | solution.py:49
  6.1 39.3 %collective-permute-start.2 = (f32[160,1152]{1,0:T(8,128)}, f32[160,1152]{1,0:T(8,128)S(1)}, u32[]{:S(2)}, u32[]{:S(2)}) collective-permute-start(f32[160,1152]{1,0:T(8,128)} %param.4), channel_id=1, source_target_pairs={{0,1},{1,0},{2,3},{3,2},{4,5},{5,4},{6,7},{7,6},{8,9},{9,8},{10,11... | collective-permute-start | bytes 2211848 | tf_op jit(solution)/shard_map/ppermute | solution.py:49
  15.0 28.5 %collective-permute-start.3 = (f32[160,1152]{1,0:T(8,128)}, f32[160,1152]{1,0:T(8,128)S(1)}, u32[]{:S(2)}, u32[]{:S(2)}) collective-permute-start(f32[160,1152]{1,0:T(8,128)} %param.5), channel_id=1, source_target_pairs={{0,4},{1,5},{2,6},{3,7},{4,8},{5,9},{6,10},{7,11},{8,12},{9,13},{1... | collective-permute-start | bytes 2211848 | tf_op jit(solution)/shard_map/ppermute | solution.py:49
  16.9 28.3 %collective-permute-start.4 = (f32[160,1152]{1,0:T(8,128)}, f32[160,1152]{1,0:T(8,128)S(1)}, u32[]{:S(2)}, u32[]{:S(2)}) collective-permute-start(f32[160,1152]{1,0:T(8,128)} %param.5), channel_id=1, source_target_pairs={{4,0},{5,1},{6,2},{7,3},{8,4},{9,5},{10,6},{11,7},{12,8},{13,9},{1... | collective-permute-start | bytes 2211848 | tf_op jit(solution)/shard_map/ppermute | solution.py:49
  32.4 12.9 %collective-permute-start.1 = (f32[160,1152]{1,0:T(8,128)S(1)}, f32[160,1152]{1,0:T(8,128)S(1)}, u32[]{:S(2)}, u32[]{:S(2)}) collective-permute-start(f32[160,1152]{1,0:T(8,128)S(1)} %collective-permute-done), channel_id=1, source_target_pairs={{0,1},{1,0},{2,3},{3,2},{4,5},{5,4},{6,7},{7,6},{8,9},{9,8},{10,11... | collective-permute-start | bytes 2211848 | tf_op jit(solution)/shard_map/ppermute | solution.py:49
  50.6 4.6 %collective-permute-start.5 = (f32[160,1152]{1,0:T(8,128)S(1)}, f32[160,1152]{1,0:T(8,128)S(1)}, u32[]{:S(2)}, u32[]{:S(2)}) collective-permute-start(f32[160,1152]{1,0:T(8,128)S(1)} %slice.38), channel_id=1, source_target_pairs={{0,1},{1,0},{2,3},{3,2},{4,5},{5,4},{6,7},{7,6},{8,9},{9,8},{10,11... | collective-permute-start | bytes 2211848 | tf_op jit(solution)/shard_map/ppermute | solution.py:49
  55.4 31.1 %collective-permute-start.7 = (f32[160,1152]{1,0:T(8,128)S(1)}, f32[160,1152]{1,0:T(8,128)S(1)}, u32[]{:S(2)}, u32[]{:S(2)}) collective-permute-start(f32[160,1152]{1,0:T(8,128)S(1)} %slice_add_fusion), channel_id=1, source_target_pairs={{0,2},{1,3},{2,0},{3,1},{48,50},{49,51},{50,48},{51,49},{96,98},{9... | collective-permute-start | bytes 2211848 | tf_op jit(solution)/shard_map/ppermute | solution.py:49
  58.7 26.0 %collective-permute-start.8 = (f32[160,1152]{1,0:T(8,128)S(1)}, f32[160,1152]{1,0:T(8,128)S(1)}, u32[]{:S(2)}, u32[]{:S(2)}) collective-permute-start(f32[160,1152]{1,0:T(8,128)S(1)} %get-tuple-element.22), channel_id=1, source_target_pairs={{0,4},{1,5},{2,6},{3,7},{4,8},{5,9},{6,10},{7,11},{8,12},{9,13},{1... | collective-permute-start | bytes 2211848 | tf_op jit(solution)/shard_map/ppermute | solution.py:49
  60.6 24.9 %collective-permute-start.9 = (f32[160,1152]{1,0:T(8,128)S(1)}, f32[160,1152]{1,0:T(8,128)S(1)}, u32[]{:S(2)}, u32[]{:S(2)}) collective-permute-start(f32[160,1152]{1,0:T(8,128)S(1)} %get-tuple-element.23), channel_id=1, source_target_pairs={{4,0},{5,1},{6,2},{7,3},{8,4},{9,5},{10,6},{11,7},{12,8},{13,9},{1... | collective-permute-start | bytes 2211848 | tf_op jit(solution)/shard_map/ppermute | solution.py:49
  70.6 15.9 %collective-permute-start.10 = (f32[160,1152]{1,0:T(8,128)S(1)}, f32[160,1152]{1,0:T(8,128)S(1)}, u32[]{:S(2)}, u32[]{:S(2)}) collective-permute-start(f32[160,1152]{1,0:T(8,128)S(1)} %slice_add_fusion), channel_id=1, source_target_pairs={{4,6},{5,7},{6,4},{7,5},{8,10},{9,11},{10,8},{11,9},{12,14},{13,15... | collective-permute-start | bytes 2211848 | tf_op jit(solution)/shard_map/ppermute | solution.py:49
  71.3 15.2 %collective-permute-start.6 = (f32[160,1152]{1,0:T(8,128)S(1)}, f32[160,1152]{1,0:T(8,128)S(1)}, u32[]{:S(2)}, u32[]{:S(2)}) collective-permute-start(f32[160,1152]{1,0:T(8,128)S(1)} %fusion.15), channel_id=1, source_target_pairs={{0,1},{1,0},{2,3},{3,2},{4,5},{5,4},{6,7},{7,6},{8,9},{9,8},{10,11... | collective-permute-start | bytes 2211848 | tf_op jit(solution)/shard_map/ppermute | solution.py:49

commit v3 on v0

--- a/solution.py
+++ b/solution.py
@@ -44,16 +44,20 @@
         far = move(photo, across)
         near = move(photo, sibling)
         far_near = move(far, sibling)
-        texts = jnp.concatenate([text, text_f, text_b], axis=0)
         p = jnp.concatenate([photo, far, far_near, near], axis=0)
         r = jnp.arange(4 * rows, dtype=jnp.int32)[:, None]
-        c = jnp.arange(3 * rows, dtype=jnp.int32)[None, :]
+        c = jnp.arange(2 * rows, dtype=jnp.int32)[None, :]
         label = jnp.where((r == c) & (r < rows), jnp.float32(1), jnp.float32(-1))
+        texts = jnp.concatenate([text, text_f], axis=0)
         logit = scale * dot(p, texts, ((1,), (1,))) + offset
         g = -label * jax.nn.sigmoid(-label * logit) * scale
+        text_b, g = lax.optimization_barrier((text_b, g))
+        logit = scale * dot(p, text_b, ((1,), (1,))) + offset
+        g = jnp.concatenate([g, jax.nn.sigmoid(logit) * scale], axis=1)
+        texts = jnp.concatenate([texts, text_b], axis=0)
         p_far = dot(g[rows : 3 * rows], texts, ((1,), (0,)))
         far_near_back = move(p_far[rows:], sibling)
-        t_fb = dot(after(g, p_far)[:, rows:], p, ((0,), (0,)))
+        t_fb = dot(g[:, rows:], p, ((0,), (0,)))
         b_back = move(t_fb[rows:], forward)
         p_across = p_far[:rows] + after(far_near_back, t_fb)
         far_back = move(p_across, across)

time: 88.9 us -> 88.8 us (level)
  waiting for transfers between devices: 21.8 us -> 20.2 us
    ppermute x10, waiting for transfers between devices: 21.8 us -> 20.2 us  [move(): return lax.ppermute(x, AXES, pairs)]
    dot_general x6 -> x7, matrix products: 11 us -> 11.8 us  [dot(): lax.dot_general(a, b, (dims, ((), ())), precision=lax.Precision.HIGH, pre...]
    unnamed x5 -> x7, local copies, waits for them, and re-layouts: 2.48 us -> 2.49 us
  transfers between devices with their start and end apart: 10 -> 10, of which waited for: 4 -> 4; matrix products, arithmetic and copies ran while one was open for 11% -> 14% of each run, Pallas kernels for 0% -> 0%
where the time goes in v3:
time: 88.8 us; the launch traced here: 88.3 us
  starting transfers between devices  49.3 us (56%)
  waiting for transfers between devices  20.2 us (23%)
  matrix products  11.8 us (13%)
  local copies, waits for them, and re-layouts  2.74 us (3%)
  between operations  2.18 us (2%)
  other arithmetic  2.14 us (2%)
    ppermute x10, starting transfers between devices, move(): return lax.ppermute(x, AXES, pairs)  49.3 us
    ppermute x10, waiting for transfers between devices, move(): return lax.ppermute(x, AXES, pairs)  20.2 us
    dot_general x7, matrix products, dot(): lax.dot_general(a, b, (dims, ((), ())), precision=lax.Precision.HIGH, pre...  11.8 us
    unnamed x7, local copies, waits for them, and re-layouts  2.49 us
    add x2, other arithmetic, shards(): return (p_own + near_back + far_back, t_own + b_back + f_back)  1.95 us
  transfers between devices with their start and end apart: 10, of which 4 were waited for; matrix products, arithmetic and copies ran while one was open for 14% of the time, Pallas kernels for 0%

profile of v3, /device:TPU:1, one launch (start us, length us, event | category | flops | bytes accessed | tf_op | source)
XLA Modules:
  0.0 88.3 jit_solution(6802066144485389410)
XLA Ops:
  0.6 5.5 %collective-permute-start.1 = (f32[160,1152]{1,0:T(8,128)}, f32[160,1152]{1,0:T(8,128)S(1)}, u32[]{:S(2)}, u32[]{:S(2)}) collective-permute-start(f32[160,1152]{1,0:T(8,128)} %param.4), channel_id=1, source_target_pairs={{0,2},{1,3},{2,0},{3,1},{4,6},{5,7},{6,4},{7,5},{8,10},{9,11},{10,... | collective-permute-start | bytes 2211848 | tf_op jit(solution)/shard_map/ppermute | solution.py:37
  6.1 8.9 %collective-permute-start.3 = (f32[160,1152]{1,0:T(8,128)}, f32[160,1152]{1,0:T(8,128)S(1)}, u32[]{:S(2)}, u32[]{:S(2)}) collective-permute-start(f32[160,1152]{1,0:T(8,128)} %param.4), channel_id=1, source_target_pairs={{0,1},{1,0},{2,3},{3,2},{4,5},{5,4},{6,7},{7,6},{8,9},{9,8},{10,11... | collective-permute-start | bytes 2211848 | tf_op jit(solution)/shard_map/ppermute | solution.py:37
  15.0 1.9 %collective-permute-start.4 = (f32[160,1152]{1,0:T(8,128)}, f32[160,1152]{1,0:T(8,128)S(1)}, u32[]{:S(2)}, u32[]{:S(2)}) collective-permute-start(f32[160,1152]{1,0:T(8,128)} %param.5), channel_id=1, source_target_pairs={{0,4},{1,5},{2,6},{3,7},{4,8},{5,9},{6,10},{7,11},{8,12},{9,13},{1... | collective-permute-start | bytes 2211848 | tf_op jit(solution)/shard_map/ppermute | solution.py:37
  16.9 11.8 %collective-permute-start = (f32[160,1152]{1,0:T(8,128)}, f32[160,1152]{1,0:T(8,128)S(1)}, u32[]{:S(2)}, u32[]{:S(2)}) collective-permute-start(f32[160,1152]{1,0:T(8,128)} %param.5), channel_id=1, source_target_pairs={{4,0},{5,1},{6,2},{7,3},{8,4},{9,5},{10,6},{11,7},{12,8},{13,9},{1... | collective-permute-start | bytes 2211848 | tf_op jit(solution)/shard_map/ppermute | solution.py:37
  30.0 1.2 %constant_dynamic-update-slice_fusion.3 = f32[640,1152]{1,0:T(8,128)S(1)} fusion(f32[160,1152]{1,0:T(8,128)} %param.4), kind=kLoop, calls=%fused_computation.43 | loop fusion | bytes 1474560
  31.2 0.0 collective-permute-done.1
  31.2 1.9 %collective-permute-start.2 = (f32[160,1152]{1,0:T(8,128)S(1)}, f32[160,1152]{1,0:T(8,128)S(1)}, u32[]{:S(2)}, u32[]{:S(2)}) collective-permute-start(f32[160,1152]{1,0:T(8,128)S(1)} %collective-permute-done.1), channel_id=1, source_target_pairs={{0,1},{1,0},{2,3},{3,2},{4,5},{5,4},{6,7},{7,6},{8,9},{9,8},{10,11... | collective-permute-start | bytes 2211848 | tf_op jit(solution)/shard_map/ppermute | solution.py:37
  33.1 1.2 %constant_dynamic-update-slice_fusion.6 = f32[480,1152]{1,0:T(8,128)S(1)} fusion(f32[160,1152]{1,0:T(8,128)} %param.5), kind=kLoop, calls=%fused_computation.46 | loop fusion | bytes 1474560
  34.3 0.1 constant_dynamic-update-slice_fusion.2
  34.4 0.0 copy-start
  34.4 9.2 %collective-permute-done.4 = f32[160,1152]{1,0:T(8,128)S(1)} collective-permute-done((f32[160,1152]{1,0:T(8,128)}, f32[160,1152]{1,0:T(8,128)S(1)}, u32[]{:S(2)}, u32[]{:S(2)}) %collective-permute-start.4) | collective-permute-done | bytes 737312 | tf_op jit(solution)/shard_map/ppermute | solution.py:37
  43.6 0.0 collective-permute-done.2
  43.6 0.1 constant_dynamic-update-slice_fusion.1
  43.7 0.0 collective-permute-done.3
  43.7 0.1 constant_dynamic-update-slice_fusion
  43.7 0.0 copy-done
  43.7 2.2 %fusion.28 = f32[640,320]{0,1:T(8,128)S(1)} fusion(f32[640,1152]{1,0:T(8,128)S(1)} %constant_dynamic-update-slice_fusion, f32[160,1152]{1,0:T(8,128)S(1)} %collective-permute-done.4, f32[160,1152]{1,0:T(8,128)S(1)} %copy-done, f32[]{:T(128)} %bitcast.12, f32[]{:T(128)} %bitcast.10, pred[640]{0:T(1024)(128)(4,1)S(1)} %iota_compare_fusion.1), kind=kOutput, calls=%fused_computation.17 | convolution fusion | flops 1418403840 | bytes 5243528 | tf_op jit(solution)/shard_map/dot_general | solution.py:26
  46.0 0.0 collective-permute-done
  46.0 0.1 constant_dynamic-update-slice_fusion.4
  46.1 1.6 %fusion.36 = f32[640,160]{0,1:T(8,128)S(1)} fusion(f32[640,1152]{1,0:T(8,128)S(1)} %constant_dynamic-update-slice_fusion, f32[160,1152]{1,0:T(8,128)S(1)} %collective-permute-done, f32[]{:T(128)} %bitcast.13, f32[]{:T(128)} %bitcast.11), kind=kOutput, calls=%fused_computation.24 | convolution fusion | flops 708403200 | bytes 4096008 | tf_op jit(solution)/shard_map/dot_general | solution.py:26
  47.7 1.9 %fusion.42 = f32[320,1152]{1,0:T(8,128)S(1)} fusion(f32[480,1152]{1,0:T(8,128)S(1)} %constant_dynamic-update-slice_fusion.4, f32[640,320]{0,1:T(8,128)S(1)} %fusion.28, f32[640,160]{0,1:T(8,128)S(1)} %fusion.36), kind=kOutput, calls=%fused_computation.30 | convolution fusion | flops 1061836800 | bytes 4915200 | tf_op jit(solution)/shard_map/dot_general | solution.py:26
  49.7 2.3 %collective-permute-start.5 = (f32[160,1152]{1,0:T(8,128)S(1)}, f32[160,1152]{1,0:T(8,128)S(1)}, u32[]{:S(2)}, u32[]{:S(2)}) collective-permute-start(f32[160,1152]{1,0:T(8,128)S(1)} %slice.39), channel_id=1, source_target_pairs={{0,1},{1,0},{2,3},{3,2},{4,5},{5,4},{6,7},{7,6},{8,9},{9,8},{10,11... | collective-permute-start | bytes 2211848 | tf_op jit(solution)/shard_map/ppermute | solution.py:37
  51.9 2.3 %fusion.38 = f32[320,1152]{1,0:T(8,128)S(1)} fusion(f32[640,1152]{1,0:T(8,128)S(1)} %constant_dynamic-update-slice_fusion, f32[640,320]{0,1:T(8,128)S(1)} %fusion.28, f32[640,160]{0,1:T(8,128)S(1)} %fusion.36), kind=kOutput, calls=%fused_computation.26 | convolution fusion | flops 1415782400 | bytes 5652480 | tf_op jit(solution)/shard_map/dot_general | solution.py:26
  54.3 0.1 fusion.53
  54.4 1.9 %collective-permute-start.7 = (f32[160,1152]{1,0:T(8,128)S(1)}, f32[160,1152]{1,0:T(8,128)S(1)}, u32[]{:S(2)}, u32[]{:S(2)}) collective-permute-start(f32[160,1152]{1,0:T(8,128)S(1)} %get-tuple-element.25), channel_id=1, source_target_pairs={{0,4},{1,5},{2,6},{3,7},{4,8},{5,9},{6,10},{7,11},{8,12},{9,13},{1... | collective-permute-start | bytes 2211848 | tf_op jit(solution)/shard_map/ppermute | solution.py:37
  56.3 0.1 pad_maximum_fusion
  56.4 0.0 collective-permute-done.5
  56.4 0.1 slice_add_fusion
  56.5 3.6 %collective-permute-start.8 = (f32[160,1152]{1,0:T(8,128)S(1)}, f32[160,1152]{1,0:T(8,128)S(1)}, u32[]{:S(2)}, u32[]{:S(2)}) collective-permute-start(f32[160,1152]{1,0:T(8,128)S(1)} %slice_add_fusion), channel_id=1, source_target_pairs={{0,2},{1,3},{2,0},{3,1},{4,6},{5,7},{6,4},{7,5},{8,10},{9,11},{10,... | collective-permute-start | bytes 2211848 | tf_op jit(solution)/shard_map/ppermute | solution.py:37
  60.1 9.4 %collective-permute-start.9 = (f32[160,1152]{1,0:T(8,128)S(1)}, f32[160,1152]{1,0:T(8,128)S(1)}, u32[]{:S(2)}, u32[]{:S(2)}) collective-permute-start(f32[160,1152]{1,0:T(8,128)S(1)} %get-tuple-element.19), channel_id=1, source_target_pairs={{4,0},{5,1},{6,2},{7,3},{8,4},{9,5},{10,6},{11,7},{12,8},{13,9},{1... | collective-permute-start | bytes 2211848 | tf_op jit(solution)/shard_map/ppermute | solution.py:37
  69.6 1.2 %fusion.46 = f32[160,1152]{1,0:T(8,128)S(1)} fusion(f32[480,1152]{1,0:T(8,128)S(1)} %constant_dynamic-update-slice_fusion.4, f32[640,480]{0,1:T(8,128)S(1)} %pad_maximum_fusion), kind=kOutput, calls=%fused_computation.36 | convolution fusion | flops 530841600 | bytes 3440640 | tf_op jit(solution)/shard_map/dot_general | solution.py:26
  70.8 2.1 %collective-permute-start.6 = (f32[160,1152]{1,0:T(8,128)S(1)}, f32[160,1152]{1,0:T(8,128)S(1)}, u32[]{:S(2)}, u32[]{:S(2)}) collective-permute-start(f32[160,1152]{1,0:T(8,128)S(1)} %fusion.46), channel_id=1, source_target_pairs={{0,1},{1,0},{2,3},{3,2},{4,5},{5,4},{6,7},{7,6},{8,9},{9,8},{10,11... | collective-permute-start | bytes 2211848 | tf_op jit(solution)/shard_map/ppermute | solution.py:37
  72.9 1.1 %fusion.44 = f32[160,1152]{1,0:T(8,128)S(1)} fusion(f32[480,1152]{1,0:T(8,128)S(1)} %constant_dynamic-update-slice_fusion.4, f32[640,480]{0,1:T(8,128)S(1)} %pad_maximum_fusion), kind=kOutput, calls=%fused_computation.34 | convolution fusion | flops 530841600 | bytes 3440640 | tf_op jit(solution)/shard_map/dot_general | solution.py:26
  74.0 1.4 %fusion.48 = f32[160,1152]{1,0:T(8,128)S(1)} fusion(f32[640,1152]{1,0:T(8,128)S(1)} %constant_dynamic-update-slice_fusion, f32[640,480]{0,1:T(8,128)S(1)} %pad_maximum_fusion), kind=kOutput, calls=%fused_computation.38 | convolution fusion | flops 707788800 | bytes 4096000 | tf_op jit(solution)/shard_map/dot_general | solution.py:26
  75.4 5.3 %collective-permute-done.7 = f32[160,1152]{1,0:T(8,128)S(1)} collective-permute-done((f32[160,1152]{1,0:T(8,128)S(1)}, f32[160,1152]{1,0:T(8,128)S(1)}, u32[]{:S(2)}, u32[]{:S(2)}) %collective-permute-start.7) | collective-permute-done | bytes 737312 | tf_op jit(solution)/shard_map/ppermute | solution.py:37
  80.6 3.9 %collective-permute-done.9 = f32[160,1152]{1,0:T(8,128)S(1)} collective-permute-done((f32[160,1152]{1,0:T(8,128)S(1)}, f32[160,1152]{1,0:T(8,128)S(1)}, u32[]{:S(2)}, u32[]{:S(2)}) %collective-permute-start.9) | collective-permute-done | bytes 737312 | tf_op jit(solution)/shard_map/ppermute | solution.py:37
  84.6 1.8 %collective-permute-done.8 = f32[160,1152]{1,0:T(8,128)S(1)} collective-permute-done((f32[160,1152]{1,0:T(8,128)S(1)}, f32[160,1152]{1,0:T(8,128)S(1)}, u32[]{:S(2)}, u32[]{:S(2)}) %collective-permute-start.8) | collective-permute-done | bytes 737312 | tf_op jit(solution)/shard_map/ppermute | solution.py:37
  86.4 1.0 %add_add_fusion = f32[160,1152]{1,0:T(8,128)} fusion(f32[160,1152]{1,0:T(8,128)S(1)} %collective-permute-done.9, f32[160,1152]{1,0:T(8,128)S(1)} %fusion.48, f32[160,1152]{1,0:T(8,128)S(1)} %collective-permute-done.7), kind=kLoop, calls=%fused_computation.32 | loop fusion | flops 368640 | bytes 2949120 | tf_op jit(solution)/shard_map/add | solution.py:72
  87.4 0.0 collective-permute-done.6
  87.4 1.0 %add_add_fusion.1 = f32[160,1152]{1,0:T(8,128)} fusion(f32[160,1152]{1,0:T(8,128)S(1)} %collective-permute-done.8, f32[160,1152]{1,0:T(8,128)S(1)} %fusion.44, f32[160,1152]{1,0:T(8,128)S(1)} %collective-permute-done.6), kind=kLoop, calls=%fused_computation.33 | loop fusion | flops 368640 | bytes 2949120 | tf_op jit(solution)/shard_map/add | solution.py:72
  (3 shorter events, 0.1 us)
Async XLA Ops:
  0.6 30.6 %collective-permute-start.1 = (f32[160,1152]{1,0:T(8,128)}, f32[160,1152]{1,0:T(8,128)S(1)}, u32[]{:S(2)}, u32[]{:S(2)}) collective-permute-start(f32[160,1152]{1,0:T(8,128)} %param.4), channel_id=1, source_target_pairs={{0,2},{1,3},{2,0},{3,1},{4,6},{5,7},{6,4},{7,5},{8,10},{9,11},{10,... | collective-permute-start | bytes 2211848 | tf_op jit(solution)/shard_map/ppermute | solution.py:37
  6.1 37.5 %collective-permute-start.3 = (f32[160,1152]{1,0:T(8,128)}, f32[160,1152]{1,0:T(8,128)S(1)}, u32[]{:S(2)}, u32[]{:S(2)}) collective-permute-start(f32[160,1152]{1,0:T(8,128)} %param.4), channel_id=1, source_target_pairs={{0,1},{1,0},{2,3},{3,2},{4,5},{5,4},{6,7},{7,6},{8,9},{9,8},{10,11... | collective-permute-start | bytes 2211848 | tf_op jit(solution)/shard_map/ppermute | solution.py:37
  15.0 28.5 %collective-permute-start.4 = (f32[160,1152]{1,0:T(8,128)}, f32[160,1152]{1,0:T(8,128)S(1)}, u32[]{:S(2)}, u32[]{:S(2)}) collective-permute-start(f32[160,1152]{1,0:T(8,128)} %param.5), channel_id=1, source_target_pairs={{0,4},{1,5},{2,6},{3,7},{4,8},{5,9},{6,10},{7,11},{8,12},{9,13},{1... | collective-permute-start | bytes 2211848 | tf_op jit(solution)/shard_map/ppermute | solution.py:37
  16.9 29.1 %collective-permute-start = (f32[160,1152]{1,0:T(8,128)}, f32[160,1152]{1,0:T(8,128)S(1)}, u32[]{:S(2)}, u32[]{:S(2)}) collective-permute-start(f32[160,1152]{1,0:T(8,128)} %param.5), channel_id=1, source_target_pairs={{4,0},{5,1},{6,2},{7,3},{8,4},{9,5},{10,6},{11,7},{12,8},{13,9},{1... | collective-permute-start | bytes 2211848 | tf_op jit(solution)/shard_map/ppermute | solution.py:37
  31.2 12.4 %collective-permute-start.2 = (f32[160,1152]{1,0:T(8,128)S(1)}, f32[160,1152]{1,0:T(8,128)S(1)}, u32[]{:S(2)}, u32[]{:S(2)}) collective-permute-start(f32[160,1152]{1,0:T(8,128)S(1)} %collective-permute-done.1), channel_id=1, source_target_pairs={{0,1},{1,0},{2,3},{3,2},{4,5},{5,4},{6,7},{7,6},{8,9},{9,8},{10,11... | collective-permute-start | bytes 2211848 | tf_op jit(solution)/shard_map/ppermute | solution.py:37
  34.4 9.4 %copy-start = (f32[160,1152]{1,0:T(8,128)S(1)}, f32[160,1152]{1,0:T(8,128)}, u32[]{:S(2)}) copy-start(f32[160,1152]{1,0:T(8,128)} %param.5) | copy-start | bytes 2211844
  49.7 6.7 %collective-permute-start.5 = (f32[160,1152]{1,0:T(8,128)S(1)}, f32[160,1152]{1,0:T(8,128)S(1)}, u32[]{:S(2)}, u32[]{:S(2)}) collective-permute-start(f32[160,1152]{1,0:T(8,128)S(1)} %slice.39), channel_id=1, source_target_pairs={{0,1},{1,0},{2,3},{3,2},{4,5},{5,4},{6,7},{7,6},{8,9},{9,8},{10,11... | collective-permute-start | bytes 2211848 | tf_op jit(solution)/shard_map/ppermute | solution.py:37
  54.4 26.3 %collective-permute-start.7 = (f32[160,1152]{1,0:T(8,128)S(1)}, f32[160,1152]{1,0:T(8,128)S(1)}, u32[]{:S(2)}, u32[]{:S(2)}) collective-permute-start(f32[160,1152]{1,0:T(8,128)S(1)} %get-tuple-element.25), channel_id=1, source_target_pairs={{0,4},{1,5},{2,6},{3,7},{4,8},{5,9},{6,10},{7,11},{8,12},{9,13},{1... | collective-permute-start | bytes 2211848 | tf_op jit(solution)/shard_map/ppermute | solution.py:37
  56.5 29.9 %collective-permute-start.8 = (f32[160,1152]{1,0:T(8,128)S(1)}, f32[160,1152]{1,0:T(8,128)S(1)}, u32[]{:S(2)}, u32[]{:S(2)}) collective-permute-start(f32[160,1152]{1,0:T(8,128)S(1)} %slice_add_fusion), channel_id=1, source_target_pairs={{0,2},{1,3},{2,0},{3,1},{4,6},{5,7},{6,4},{7,5},{8,10},{9,11},{10,... | collective-permute-start | bytes 2211848 | tf_op jit(solution)/shard_map/ppermute | solution.py:37
  60.1 24.4 %collective-permute-start.9 = (f32[160,1152]{1,0:T(8,128)S(1)}, f32[160,1152]{1,0:T(8,128)S(1)}, u32[]{:S(2)}, u32[]{:S(2)}) collective-permute-start(f32[160,1152]{1,0:T(8,128)S(1)} %get-tuple-element.19), channel_id=1, source_target_pairs={{4,0},{5,1},{6,2},{7,3},{8,4},{9,5},{10,6},{11,7},{12,8},{13,9},{1... | collective-permute-start | bytes 2211848 | tf_op jit(solution)/shard_map/ppermute | solution.py:37
  70.8 16.6 %collective-permute-start.6 = (f32[160,1152]{1,0:T(8,128)S(1)}, f32[160,1152]{1,0:T(8,128)S(1)}, u32[]{:S(2)}, u32[]{:S(2)}) collective-permute-start(f32[160,1152]{1,0:T(8,128)S(1)} %fusion.46), channel_id=1, source_target_pairs={{0,1},{1,0},{2,3},{3,2},{4,5},{5,4},{6,7},{7,6},{8,9},{9,8},{10,11... | collective-permute-start | bytes 2211848 | tf_op jit(solution)/shard_map/ppermute | solution.py:37
